TPU v7x, 1024 devices: a whole 8x8x8 slice. The times are simulated.
1024 devices in a mesh: tm: 256 (over y, x_lo, z), mp: 4 (over x_hi, core).
Axes of the slice: x: 8 (x_hi: 2, x_lo: 4; x = x_hi * 4 + x_lo), y: 8, z: 8, core: 2. Of those that a mesh axis runs over, the one named last changes fastest.
Arguments:
- frames: bfloat16 [65536, 1536], P('tm', 'mp'), may hold values from -6 to 6
- ffn_gain: float32 [1536], replicated, may hold values from 0.2 to 5
- w_up: bfloat16 [1536, 3072], P(None, 'mp'), may hold values from -0.15625 to 0.15625
- w_down: bfloat16 [3072, 1536], P('mp'), may hold values from -0.21875 to 0.21875
- ln_gain: float32 [1536], replicated, may hold values from 0.25 to 1.75
- w_qkv: bfloat16 [1536, 3, 1536], P(None, None, 'mp')
- w_out: bfloat16 [1536, 1536], P('mp'), may hold values from -0.3125 to 0.3125
- conv_kernel: float32 [31, 1536], P(None, 'mp'), may hold values from -2 to 2
- left_groups: int32 [256], P('tm'), may hold values from 0 to 3, as said below
- start_offset: int32 [256], P('tm'), may hold values from 0 to 127
Outputs:
- block_out: bfloat16 [65536, 1536], P('tm', 'mp')
Inputs may be any that keep to these rules, and one draw needn't show every extreme that they name: left_groups[c] is at most the number of groups of c's recording that lie before c: context never crosses a recording.
All inputs are finite; a program needn't handle non-finite values.
Results may differ from a plain program's by a relative error of at most 0.04.
Values may be sent and summed in bfloat16 or wider, within the bound.
A program may use at most 64 MiB of HBM per device.

v0:
```python
import jax
import jax.numpy as jnp
from jax import lax
from jax.sharding import PartitionSpec as P

HEAD_DIM = 64
KERNEL = 31
LEFT = 3
REC_SHARDS = 8


def from_behind(block, axis, distance):
    devices = range(lax.axis_size(axis))
    route = [(i - distance, i) for i in devices if i - distance in devices]
    return lax.ppermute(block, axis, route)


def padded_2(x, sides, width):
    for axis, dim in sides:
        peers, length = (lax.axis_size(axis), x.shape[dim])
        up = [(i, (i + 1) % peers) for i in range(peers - 1)]
        down = [(j, i) for i, j in up]
        last = lax.slice_in_dim(x, length - width, length, axis=dim)
        first = lax.slice_in_dim(x, 0, width, axis=dim)
        before = lax.ppermute(last, axis, up)
        after = lax.ppermute(first, axis, down)
        x = jnp.concatenate([before, x, after], axis=dim)
    return x


def layer_norm(values_in, gain):
    widened = values_in.astype(jnp.float32)
    center = jnp.mean(widened, axis=-1, keepdims=True)
    spread = jnp.mean((widened - center) ** 2, axis=-1, keepdims=True)
    return ((widened - center) * lax.rsqrt(spread + 1e-05) * gain).astype(jnp.bfloat16)


def body(
    frames, ffn_gain, w_up, w_down, ln_gain, w_qkv, w_out, conv_kernel, left_groups, start_offset
):
    rows_here = frames.shape[0]
    local_width = frames.shape[1]
    head_count = local_width // HEAD_DIM
    whole = lax.all_gather(frames, "mp", axis=1, tiled=True)
    ffn_normed = layer_norm(whole, ffn_gain)
    ffn_hidden = jax.nn.silu(jnp.dot(ffn_normed, w_up, preferred_element_type=jnp.float32)).astype(
        jnp.bfloat16
    )
    partial_sum = jnp.dot(ffn_hidden, w_down, preferred_element_type=jnp.float32)
    shares = lax.psum_scatter(
        partial_sum.astype(jnp.bfloat16), "mp", scatter_dimension=1, tiled=True
    ).astype(jnp.float32)
    ffn_mid = (frames.astype(jnp.float32) + 0.5 * shares).astype(jnp.bfloat16)
    mixed_all = lax.all_gather(ffn_mid, "mp", axis=1, tiled=True)
    normed = layer_norm(mixed_all, ln_gain)
    projected = jnp.dot(
        normed, w_qkv.reshape(w_qkv.shape[0], 3 * local_width), preferred_element_type=jnp.float32
    ).astype(jnp.bfloat16)
    queries = projected[:, :local_width].reshape(rows_here, head_count, HEAD_DIM)
    key_value = projected[:, local_width:]
    moving = key_value
    earlier = []
    for hop_index in range(LEFT):
        moving = from_behind(moving, "tm", 1)
        earlier.insert(0, moving)
    window = jnp.concatenate(earlier + [key_value], axis=0)
    keys = window[:, :local_width].reshape(-1, head_count, HEAD_DIM)
    values = window[:, local_width:].reshape(-1, head_count, HEAD_DIM)
    key_index = jnp.arange((LEFT + 1) * rows_here, dtype=jnp.int32)
    distance = LEFT - key_index // rows_here
    position = key_index % rows_here
    left_count = left_groups[0]
    offset = start_offset[0]
    visible = (distance < left_count) | (distance == left_count) & (
        (left_count == 0) | (position >= offset)
    )
    scores = jnp.einsum(
        "thd,jhd->htj", queries, keys, preferred_element_type=jnp.float32
    ) * HEAD_DIM ** (-0.5)
    scores = jnp.where(visible[None, None, :], scores, -jnp.inf)
    highest = jnp.max(scores, axis=-1, keepdims=True)
    expo = jnp.where(visible[None, None, :], jnp.exp(scores - highest), 0.0)
    attn_weights = (expo / jnp.sum(expo, axis=-1, keepdims=True)).astype(jnp.bfloat16)
    context_cols = jnp.einsum(
        "htj,jhd->hdt", attn_weights, values, preferred_element_type=jnp.float32
    )
    context_cols = context_cols.astype(jnp.bfloat16).reshape(local_width, rows_here)
    attn_channels = lax.psum_scatter(
        lax.dot_general(
            w_out, context_cols, (((0,), (0,)), ((), ())), preferred_element_type=jnp.float32
        ).astype(jnp.bfloat16),
        "mp",
        scatter_dimension=0,
        tiled=True,
    ).astype(jnp.float32)
    mid_channels = (ffn_mid.T.astype(jnp.float32) + attn_channels).astype(jnp.bfloat16)
    half = (KERNEL - 1) // 2
    padded = padded_2(mid_channels, (("tm", 1),), half)
    place = lax.axis_index("tm") % REC_SHARDS
    rec_start = place == REC_SHARDS // 2
    rec_end = place == REC_SHARDS // 2 - 1
    column = jnp.arange(rows_here + 2 * half, dtype=jnp.int32)
    rim_keep = ((column >= half) | jnp.logical_not(rec_start)) & (
        (column < rows_here + half) | jnp.logical_not(rec_end)
    )
    padded = jnp.where(rim_keep[None, :], padded.astype(jnp.float32), 0.0)
    accumulated = jnp.zeros((local_width, rows_here), jnp.float32)
    for tap_index in range(KERNEL):
        accumulated = (
            accumulated
            + conv_kernel[tap_index][:, None] * padded[:, tap_index : tap_index + rows_here]
        )
    result = mid_channels.astype(jnp.float32) + jax.nn.silu(accumulated)
    return result.T.astype(jnp.bfloat16)


def solution(mesh):
    return jax.shard_map(
        body,
        mesh=mesh,
        in_specs=(
            P("tm", "mp"),
            P(),
            P(None, "mp"),
            P("mp", None),
            P(),
            P(None, None, "mp"),
            P("mp", None),
            P(None, "mp"),
            P("tm"),
            P("tm"),
        ),
        out_specs=P("tm", "mp"),
        check_vma=False,
    )
```

profile of v0, /device:TPU:80, one launch (start us, length us, event | category | flops | bytes accessed | tf_op | source)
XLA Modules:
  0.0 254.7 jit_solution(16112257890760412835)
XLA Ops:
  6.5 0.0 copy-start
  6.5 0.0 copy-start.7
  6.5 0.0 reduce-scatter.7.cloned.1.call-start
  6.5 15.4 %all_gather.6 = bf16[256,1536]{1,0:T(8,128)(2,1)S(1)} all-gather(bf16[256,384]{1,0:T(8,128)(2,1)} %param.10), channel_id=1, replica_groups=mesh['tm'=256,'mp'=4] {'mp'}, dimensions={1}, use_global_device_ids=true | all-gather | bytes 983040 | tf_op jit(solution)/shard_map/all_gather | solution.py:44
  22.0 0.2 convert_reduce_fusion.1
  22.1 0.3 fusion.14
  22.5 0.0 copy-done
  22.5 0.0 copy-done.7
  22.5 4.3 %convolution_convert_fusion.1 = bf16[256,1536]{1,0:T(8,128)(2,1)} fusion(bf16[768,1536]{1,0:T(8,128)(2,1)S(1)} %copy-done, bf16[1536,768]{1,0:T(8,128)(2,1)} %param.12, bf16[256,1536]{1,0:T(8,128)(2,1)S(1)} %all_gather.6, f32[1536]{0:T(1024)S(1)} %copy-done.7, f32[256]{0:T(256)S(1)} %add_rsqrt_fusion.1, f32[256]{0:T(256)S(1)} %broadcast_multiply_fusion.1), kind=kOutput, calls=%fused_computation.10 | convolution fusion | flops 1211301888 | bytes 6299648 | tf_op jit(solution)/shard_map/dot_general | solution.py:49
  26.9 2.3 copy.22
  29.2 0.0 reduce-scatter.7.cloned.1.call-update
  29.2 0.0 copy-start.3
  29.2 0.0 reduce-scatter.9.cloned.1.call-start
  29.2 6.1 %copy.18 = bf16[1536,3,384]{0,2,1:T(8,128)(2,1)} copy(bf16[1536,3,384]{2,0,1:T(8,128)(2,1)} %param.15) | data formatting | bytes 7077888 | tf_op args[5]
  35.4 55.7 %reduce-scatter.7.cloned.1.call-done = bf16[384,256]{1,0:T(8,128)(2,1)} async-done(((bf16[1536,256]{1,0:T(8,128)(2,1)}), bf16[384,256]{1,0:T(8,128)(2,1)}) %reduce-scatter.7.cloned.1.call-update) | async-done | bytes 196624
  91.1 1.1 copy.23
  92.2 0.0 copy-done.3
  92.2 0.0 copy-start.8
  92.2 0.1 add_convert_fusion.1
  92.3 12.2 %all_gather.7 = bf16[256,1536]{1,0:T(8,128)(2,1)S(1)} all-gather(bf16[256,384]{1,0:T(8,128)(2,1)S(1)} %add_convert_fusion.1), channel_id=1, replica_groups=mesh['tm'=256,'mp'=4] {'mp'}, dimensions={1}, use_global_device_ids=true | all-gather | bytes 983040 | tf_op jit(solution)/shard_map/all_gather | solution.py:54
  104.5 0.2 convert_reduce_fusion
  104.6 0.3 fusion.11
  105.0 0.0 copy-done.8
  105.0 3.3 %convolution_convert_fusion = bf16[256,1152]{1,0:T(8,128)(2,1)S(1)} fusion(bf16[1536,1152]{0,1:T(8,128)(2,1)} %bitcast.31, bf16[256,1536]{1,0:T(8,128)(2,1)S(1)} %all_gather.7, f32[1536]{0:T(1024)S(1)} %copy-done.8, f32[256]{0:T(256)S(1)} %add_rsqrt_fusion, f32[256]{0:T(256)S(1)} %broadcast_multiply_fusion), kind=kOutput, calls=%fused_computation.9 | convolution fusion | flops 908230656 | bytes 4923392 | tf_op jit(solution)/shard_map/dot_general | solution.py:56
  108.3 0.0 copy-start.4
  108.4 3.7 %collective-permute-start = (bf16[256,768]{1,0:T(8,128)(2,1)S(1)}, bf16[256,768]{1,0:T(8,128)(2,1)S(1)}, u32[]{:S(2)}, u32[]{:S(2)}) collective-permute-start(bf16[256,768]{1,0:T(8,128)(2,1)S(1)} %slice.272), channel_id=1, source_target_pairs={{0,4},{4,8},{8,12},{12,16},{16,20},{20,24},{24,28},{28,32},{32,36}... | collective-permute-start | bytes 1179656 | tf_op jit(solution)/shard_map/ppermute | solution.py:15
  112.1 14.8 %collective-permute-done = bf16[256,768]{1,0:T(8,128)(2,1)S(1)} collective-permute-done((bf16[256,768]{1,0:T(8,128)(2,1)S(1)}, bf16[256,768]{1,0:T(8,128)(2,1)S(1)}, u32[]{:S(2)}, u32[]{:S(2)}) %collective-permute-start) | collective-permute-done | bytes 393248 | tf_op jit(solution)/shard_map/ppermute | solution.py:15
  126.9 0.0 copy-done.4
  126.9 1.9 collective-permute-start.1
  128.8 15.7 %collective-permute-done.1 = bf16[256,768]{1,0:T(8,128)(2,1)} collective-permute-done((bf16[256,768]{1,0:T(8,128)(2,1)S(1)}, bf16[256,768]{1,0:T(8,128)(2,1)}, u32[]{:S(2)}, u32[]{:S(2)}) %collective-permute-start.1) | collective-permute-done | bytes 393248 | tf_op jit(solution)/shard_map/ppermute | solution.py:15
  144.5 1.9 collective-permute-start.2
  147.7 0.9 slice.274
  148.7 0.8 copy.20
  149.5 11.9 %collective-permute-done.2 = bf16[256,768]{1,0:T(8,128)(2,1)} collective-permute-done((bf16[256,768]{1,0:T(8,128)(2,1)}, bf16[256,768]{1,0:T(8,128)(2,1)}, u32[]{:S(2)}, u32[]{:S(2)}) %collective-permute-start.2) | collective-permute-done | bytes 393248 | tf_op jit(solution)/shard_map/ppermute | solution.py:15
  161.4 1.2 pad_maximum_fusion
  162.7 1.0 fusion.89
  163.7 0.0 copy-start.5
  163.7 2.3 copy.19
  166.0 1.2 copy.21
  167.2 0.0 copy-done.5
  167.2 0.0 copy-start.2
  167.2 6.1 %fusion.91 = (f32[6,256]{1,0:T(8,128)S(1)}, f32[6,256,1024]{2,1,0:T(8,128)}) fusion(pred[1024]{0:T(1024)(128)(4,1)S(1)} %fusion.80, bf16[256,6,64]{0,2,1:T(8,128)(2,1)S(1)} %bitcast.36, bf16[1024,6,64]{0,2,1:T(8,128)(2,1)} %bitcast.34), kind=kOutput, calls=%fused_computation.169 | convolution fusion | flops 209191936 | bytes 7281664 | tf_op jit(solution)/shard_map/sub | solution.py:82
  173.3 0.0 copy-done.2
  173.3 0.0 copy-start.1
  173.3 4.0 %fusion.17 = bf16[6,64,256]{2,1,0:T(8,128)(2,1)S(1)} fusion(bf16[1024,6,64]{0,2,1:T(8,128)(2,1)S(1)} %bitcast.33, f32[6,256,1024]{2,1,0:T(8,128)} %get-tuple-element.41, f32[6,256]{1,0:T(8,128)S(1)} %get-tuple-element.40), kind=kOutput, calls=%fused_computation.28 | convolution fusion | flops 204570624 | bytes 7280640 | tf_op jit(solution)/shard_map/htj,jhd->hdt/dot_general | solution.py:84
  177.3 0.0 copy-done.1
  177.3 0.6 fusion.6
  177.9 0.0 copy-start.6
  178.0 1.2 copy.24
  179.1 0.0 reduce-scatter.9.cloned.1.call-update
  179.2 0.0 copy-done.6
  179.2 0.1 slice_reduce_fusion.29
  179.2 0.1 slice_reduce_fusion.30
  179.3 45.1 %reduce-scatter.9.cloned.1.call-done = bf16[384,256]{1,0:T(8,128)(2,1)} async-done(((bf16[1536,256]{1,0:T(8,128)(2,1)}), bf16[384,256]{1,0:T(8,128)(2,1)}) %reduce-scatter.9.cloned.1.call-update) | async-done | bytes 196624
  224.4 1.1 copy.25
  225.5 0.1 fusion.66
  225.6 9.9 %collective-permute-start.4 = (bf16[384,15]{0,1:T(8,128)(2,1)S(1)}, bf16[384,15]{0,1:T(8,128)(2,1)S(1)}, u32[]{:S(2)}, u32[]{:S(2)}) collective-permute-start(bf16[384,15]{0,1:T(8,128)(2,1)S(1)} %get-tuple-element.39), channel_id=1, source_target_pairs={{4,0},{8,4},{12,8},{16,12},{20,16},{24,20},{28,24},{32,28},{36,32}... | collective-permute-start | bytes 34568 | tf_op jit(solution)/shard_map/ppermute | solution.py:26
  235.5 1.9 collective-permute-start.3
  237.5 0.0 collective-permute-done.4
  237.5 8.4 %collective-permute-done.3 = bf16[384,15]{0,1:T(8,128)(2,1)S(1)} collective-permute-done((bf16[384,15]{0,1:T(8,128)(2,1)S(1)}, bf16[384,15]{0,1:T(8,128)(2,1)S(1)}, u32[]{:S(2)}, u32[]{:S(2)}) %collective-permute-start.3) | collective-permute-done | bytes 11552 | tf_op jit(solution)/shard_map/ppermute | solution.py:25
  245.9 0.1 convert_select_fusion
  246.0 1.8 fusion.68
  (8 shorter events, 0.1 us)
Async XLA Ops:
  6.5 16.0 %copy-start = (bf16[768,1536]{1,0:T(8,128)(2,1)S(1)}, bf16[768,1536]{1,0:T(8,128)(2,1)}, u32[]{:S(2)}) copy-start(bf16[768,1536]{1,0:T(8,128)(2,1)} %param.13) | copy-start | bytes 7077892
  6.5 16.0 %copy-start.7 = (f32[1536]{0:T(1024)S(1)}, f32[1536]{0:T(1024)}, u32[]{:S(2)}) copy-start(f32[1536]{0:T(1024)} %param.11) | copy-start | bytes 18436
  6.5 84.5 %reduce-scatter.7.cloned.1.call-start = ((), (), s32[]{:S(2)}) async-start(), calls=%async_computation.2 | async-start | bytes 983040
  29.2 63.0 %copy-start.3 = (bf16[256,384]{1,0:T(8,128)(2,1)S(1)}, bf16[256,384]{1,0:T(8,128)(2,1)}, u32[]{:S(2)}) copy-start(bf16[256,384]{1,0:T(8,128)(2,1)} %param.10) | copy-start | bytes 589828
  29.2 195.3 %reduce-scatter.9.cloned.1.call-start = ((), (), s32[]{:S(2)}) async-start(), calls=%async_computation.3 | async-start | bytes 983040
  92.2 12.8 %copy-start.8 = (f32[1536]{0:T(1024)S(1)}, f32[1536]{0:T(1024)}, u32[]{:S(2)}) copy-start(f32[1536]{0:T(1024)} %param.14) | copy-start | bytes 18436
  108.3 18.6 %copy-start.4 = (bf16[256,1152]{1,0:T(8,128)(2,1)}, bf16[256,1152]{1,0:T(8,128)(2,1)S(1)}, u32[]{:S(2)}) copy-start(bf16[256,1152]{1,0:T(8,128)(2,1)S(1)} %convolution_convert_fusion) | copy-start | bytes 1769476
  108.4 18.6 %collective-permute-start = (bf16[256,768]{1,0:T(8,128)(2,1)S(1)}, bf16[256,768]{1,0:T(8,128)(2,1)S(1)}, u32[]{:S(2)}, u32[]{:S(2)}) collective-permute-start(bf16[256,768]{1,0:T(8,128)(2,1)S(1)} %slice.272), channel_id=1, source_target_pairs={{0,4},{4,8},{8,12},{12,16},{16,20},{20,24},{24,28},{28,32},{32,36}... | collective-permute-start | bytes 1179656 | tf_op jit(solution)/shard_map/ppermute | solution.py:15
  126.9 17.6 %collective-permute-start.1 = (bf16[256,768]{1,0:T(8,128)(2,1)S(1)}, bf16[256,768]{1,0:T(8,128)(2,1)}, u32[]{:S(2)}, u32[]{:S(2)}) collective-permute-start(bf16[256,768]{1,0:T(8,128)(2,1)S(1)} %collective-permute-done), channel_id=1, source_target_pairs={{0,4},{4,8},{8,12},{12,16},{16,20},{20,24},{24,28},{28,32},{32,36}... | collective-permute-start | bytes 1179656 | tf_op jit(solution)/shard_map/ppermute | solution.py:15
  144.5 16.9 %collective-permute-start.2 = (bf16[256,768]{1,0:T(8,128)(2,1)}, bf16[256,768]{1,0:T(8,128)(2,1)}, u32[]{:S(2)}, u32[]{:S(2)}) collective-permute-start(bf16[256,768]{1,0:T(8,128)(2,1)} %collective-permute-done.1), channel_id=1, source_target_pairs={{0,4},{4,8},{8,12},{12,16},{16,20},{20,24},{24,28},{28,32},{32,36}... | collective-permute-start | bytes 1179656 | tf_op jit(solution)/shard_map/ppermute | solution.py:15
  163.7 3.5 %copy-start.5 = (bf16[256,384]{0,1:T(8,128)(2,1)S(1)}, bf16[256,384]{0,1:T(8,128)(2,1)}, u32[]{:S(2)}) copy-start(bf16[256,384]{0,1:T(8,128)(2,1)} %copy.20) | copy-start | bytes 589828
  167.2 6.1 %copy-start.2 = (bf16[1024,384]{0,1:T(8,128)(2,1)S(1)}, bf16[1024,384]{0,1:T(8,128)(2,1)}, u32[]{:S(2)}) copy-start(bf16[1024,384]{0,1:T(8,128)(2,1)} %copy.19) | copy-start | bytes 2359300
  173.3 4.0 %copy-start.1 = (bf16[384,1536]{1,0:T(8,128)(2,1)S(1)}, bf16[384,1536]{1,0:T(8,128)(2,1)}, u32[]{:S(2)}) copy-start(bf16[384,1536]{1,0:T(8,128)(2,1)} %param.16) | copy-start | bytes 3538948
  177.9 1.2 copy-start.6
  225.6 11.9 %collective-permute-start.4 = (bf16[384,15]{0,1:T(8,128)(2,1)S(1)}, bf16[384,15]{0,1:T(8,128)(2,1)S(1)}, u32[]{:S(2)}, u32[]{:S(2)}) collective-permute-start(bf16[384,15]{0,1:T(8,128)(2,1)S(1)} %get-tuple-element.39), channel_id=1, source_target_pairs={{4,0},{8,4},{12,8},{16,12},{20,16},{24,20},{28,24},{32,28},{36,32}... | collective-permute-start | bytes 34568 | tf_op jit(solution)/shard_map/ppermute | solution.py:26
  235.5 10.4 %collective-permute-start.3 = (bf16[384,15]{0,1:T(8,128)(2,1)S(1)}, bf16[384,15]{0,1:T(8,128)(2,1)S(1)}, u32[]{:S(2)}, u32[]{:S(2)}) collective-permute-start(bf16[384,15]{0,1:T(8,128)(2,1)S(1)} %get-tuple-element.38), channel_id=1, source_target_pairs={{0,4},{4,8},{8,12},{12,16},{16,20},{20,24},{24,28},{28,32},{32,36}... | collective-permute-start | bytes 34568 | tf_op jit(solution)/shard_map/ppermute | solution.py:25
Sparse Core Ops, SparseCore 0:
  29.3 61.7 reduce-scatter.6
  179.3 45.1 reduce-scatter.8
where the time goes:
time: 256 us; the launch traced here: 255 us
  waiting for transfers between devices  152 us (59%)
  blocking collectives  27.6 us (11%)
  starting transfers between devices  19.4 us (8%)
  local copies, waits for them, and re-layouts  18.3 us (7%)
  matrix products  18.3 us (7%)
  between operations  15 us (6%)
  other arithmetic  4.38 us (2%)
    unnamed x4, waiting for transfers between devices  101 us
    ppermute x3, waiting for transfers between devices, from_behind(): return lax.ppermute(block, axis, route)  42.4 us
    all_gather x1, blocking collectives, body(): whole = lax.all_gather(frames, 'mp', axis=1, tiled=True)  15.4 us
    all_gather x1, blocking collectives, body(): mixed_all = lax.all_gather(ffn_mid, 'mp', axis=1, tiled=True)  12.2 us
    unnamed x23, local copies, waits for them, and re-layouts  11.8 us
    ppermute x1, starting transfers between devices, padded_2(): after = lax.ppermute(first, axis, down)  9.9 us
    ppermute x1, waiting for transfers between devices, padded_2(): before = lax.ppermute(last, axis, up)  8.44 us
    ppermute x3, starting transfers between devices, from_behind(): return lax.ppermute(block, axis, route)  7.55 us
  transfers between devices with their start and end apart: 7, of which 6 were waited for; matrix products, arithmetic and copies ran while one was open for 3% of the time, Pallas kernels for 0%

commit v1 on v0

v1 whole, which is shorter than its diff:
```python
import functools

import jax
import jax.numpy as jnp
from jax import lax
from jax.experimental import pallas as pl
from jax.experimental.pallas import tpu as pltpu
from jax.sharding import PartitionSpec as P

HEAD_DIM = 64
KERNEL = 31
LEFT = 3
REC_SHARDS = 8
CHUNKS = 2
LANES = 128
HALO = 16
HIDDEN_STEP = 256
NEVER = -1e30
F32 = jnp.float32
BF16 = jnp.bfloat16


def layer_norm(values_in, gain):
    widened = values_in.astype(F32)
    center = jnp.mean(widened, axis=-1, keepdims=True)
    shifted = widened - center
    spread = jnp.mean(shifted * shifted, axis=-1, keepdims=True)
    return (shifted * lax.rsqrt(spread + 1e-05) * gain).astype(BF16)


def dot(a, b, dims=((1,), (0,))):
    return lax.dot_general(a, b, (dims, ((), ())), preferred_element_type=F32)


def block_kernel(
    left_ref, offset_ref, frames, ffn_gain, w_up, w_down, ln_gain, w_qkv, w_out, taps, out,
    whole, up_v, down_v, qkv_v, out_v, hidden, normed, partial, partial_in, chip_out, chip_in,
    ffn_mid, queries, kv, scores, context, proj, proj_in, cross_out, cross_in, padded,
    edge_out, edge_in, local_sem, send_sem, recv_sem,
):
    rows, width = frames.shape
    d_model = whole.shape[1]
    size = rows // CHUNKS
    half = size // 2
    groups = lax.axis_size("tm")
    group = lax.axis_index("tm")
    me = lax.axis_index("mp")
    core = lax.rem(me, 2)
    side = me // 2
    sibling = me + 1 - 2 * core
    partner = lax.rem(me + 2, 4)
    following = lax.rem(group + 1, groups)
    previous = lax.rem(group + groups - 1, groups)

    loads = []
    for i, (src, dst) in enumerate(
        ((w_up, up_v), (w_down, down_v), (w_qkv, qkv_v), (w_out, out_v))
    ):
        loads.append(pltpu.make_async_copy(src, dst, local_sem.at[i]))
    own_cols = pl.ds(pl.multiple_of(me * width, LANES), width)
    own_frames = pltpu.make_async_copy(frames, whole.at[:, own_cols], local_sem.at[4])
    own_frames.start()
    for load in loads:
        load.start()

    barrier = pltpu.get_barrier_semaphore()
    for target in ({"mp": sibling}, {"mp": partner}, {"tm": following}, {"tm": previous}):
        pl.semaphore_signal(
            barrier, inc=1, device_id=target, device_id_type=pl.DeviceIdType.MESH
        )
    pl.semaphore_wait(barrier, 4)

    copies = []

    def send(src, dst, target):
        i = len(copies)
        copy = pltpu.make_async_remote_copy(
            src_ref=src, dst_ref=dst, send_sem=send_sem.at[i], recv_sem=recv_sem.at[i],
            device_id=target, device_id_type=pl.DeviceIdType.MESH,
        )
        copies.append(copy)
        copy.start()
        return copy

    def span(r):
        return pl.ds(r * size, size)

    def shared(r):
        return pl.ds(pl.multiple_of(r * size + core * half, half), half)

    to_partner, to_sibling = [], []
    for r in range(CHUNKS):
        to_partner.append(
            send(frames.at[span(r), :], whole.at[span(r), own_cols], {"mp": partner})
        )
        to_sibling.append(
            send(frames.at[span(r), :], whole.at[span(r), own_cols], {"mp": sibling})
        )
    own_frames.wait()

    partner_cols = pl.ds(pl.multiple_of(partner * width, LANES), width)
    crossing = []
    for r in range(CHUNKS):
        to_partner[r].wait_recv()
        passed_on = send(
            whole.at[span(r), partner_cols], whole.at[span(r), partner_cols], {"mp": sibling}
        )
        to_sibling[r].wait_recv()
        passed_on.wait_recv()
        normed[...] = layer_norm(whole[span(r), :], ffn_gain[...])
        if r == 0:
            loads[0].wait()

        @pl.loop(0, up_v.shape[1] // HIDDEN_STEP)
        def _(j):
            cols = pl.ds(pl.multiple_of(j * HIDDEN_STEP, HIDDEN_STEP), HIDDEN_STEP)
            v = dot(normed[...], up_v[:, cols])
            hidden[:, cols] = (v / (1.0 + jnp.exp(-v))).astype(BF16)

        if r == 0:
            loads[1].wait()

        @pl.loop(0, d_model // HIDDEN_STEP)
        def _(j):
            cols = pl.ds(pl.multiple_of(j * HIDDEN_STEP, HIDDEN_STEP), HIDDEN_STEP)
            partial[r, :, cols] = dot(hidden[...], down_v[:, cols]).astype(BF16)

        mine = pl.ds(pl.multiple_of(core * half, half), half)
        theirs = pl.ds(pl.multiple_of((1 - core) * half, half), half)
        swap = send(partial.at[r, theirs, :], partial_in.at[r], {"mp": sibling})
        swap.wait_recv()
        chip_out[r] = (partial[r, mine, :].astype(F32) + partial_in[r].astype(F32)).astype(BF16)
        crossing.append(send(chip_out.at[r], chip_in.at[r], {"mp": partner}))

    hops = {}

    def hop(h, r):
        if h > 1:
            hops[h - 1, r].wait_recv()
        hops[h, r] = send(kv.at[h - 1, span(r), :], kv.at[h, span(r), :], {"tm": following})

    for r in range(CHUNKS):
        crossing[r].wait_recv()
        total = chip_out[r].astype(F32) + chip_in[r].astype(F32)
        ffn_mid[shared(r), :] = (whole[shared(r), :].astype(F32) + 0.5 * total).astype(BF16)
        joined = send(ffn_mid.at[shared(r), :], ffn_mid.at[shared(r), :], {"mp": sibling})
        joined.wait_recv()
        normed[...] = layer_norm(ffn_mid[span(r), :], ln_gain[...])
        if r == 0:
            loads[2].wait()
        for c in (1, 2):
            cols = slice(c * width, (c + 1) * width)
            kv[0, span(r), slice((c - 1) * width, c * width)] = dot(
                normed[...], qkv_v[:, cols]
            ).astype(BF16)
        hop(1, r)
        queries[span(r), :] = (
            dot(normed[...], qkv_v[:, 0:width]).astype(BF16) * (HEAD_DIM ** -0.5)
        ).astype(BF16)
        for h in range(2, LEFT + 1):
            if r - h + 1 >= 0:
                hop(h, r - h + 1)

    left = left_ref[0]
    offset = offset_ref[0]
    position = lax.broadcasted_iota(jnp.int32, (rows, rows), 1)
    upper = lax.broadcasted_iota(jnp.int32, (rows, LANES), 1) >= HEAD_DIM

    def score(d):
        if d > 0:
            first = jnp.where(d < left, 0, jnp.where(d == left, offset, rows))
            shown = position >= first

        @pl.loop(0, width // LANES)
        def _(p):
            cols = pl.ds(pl.multiple_of(p * LANES, LANES), LANES)
            pair = queries[:, cols]
            keys = kv[d, :, cols]
            for odd in range(2):
                picked = jnp.where(upper if odd else jnp.logical_not(upper), pair, 0)
                s = dot(picked, keys, ((1,), (1,)))
                if d > 0:
                    s = jnp.where(shown, s, NEVER)
                scores[2 * p + odd, :, d * rows : (d + 1) * rows] = s

    todo = [(h, r) for r in range(CHUNKS) for h in range(2, LEFT + 1) if r + h - 1 >= CHUNKS]
    todo.sort(key=lambda item: (item[0] + item[1], item[1]))
    late = [item for item in todo if item[0] + item[1] <= CHUNKS]
    for item in late:
        hop(*item)
    score(0)
    rest = [item for item in todo if item not in late]
    for d in range(1, LEFT + 1):
        for item in [i for i in rest if i[0] + i[1] == CHUNKS + d]:
            hop(*item)
        for r in range(CHUNKS):
            if (d + 1, r) not in hops:
                hops[d, r].wait_recv()
        score(d)

    lower = lax.broadcasted_iota(jnp.int32, (size, LANES), 1) < HEAD_DIM
    swaps, outgoing = [], []
    loads[3].wait()
    for r in range(CHUNKS):

        @pl.loop(0, width // LANES)
        def _(p):
            cols = pl.ds(pl.multiple_of(p * LANES, LANES), LANES)
            val_cols = pl.ds(pl.multiple_of(width + p * LANES, LANES), LANES)
            found = []
            for odd in range(2):
                s = scores[2 * p + odd, span(r), :]
                e = jnp.exp(s - jnp.max(s, axis=-1, keepdims=True))
                norm = jnp.sum(e, axis=-1, keepdims=True)
                e = e.astype(BF16)
                acc = None
                for d in range(LEFT + 1):
                    term = dot(e[:, d * rows : (d + 1) * rows], kv[d, :, val_cols])
                    acc = term if acc is None else acc + term
                found.append(acc / norm)
            context[span(r), cols] = jnp.where(lower, found[0], found[1]).astype(BF16)

        for k in range(4):
            proj[r, (k % 2) * 2 + k // 2] = dot(
                context[span(r), :], out_v[:, k * width : (k + 1) * width]
            ).astype(BF16)
        swap = send(
            proj.at[r, pl.ds((1 - core) * 2, 2)], proj_in.at[r], {"mp": sibling}
        )
        swap.wait_recv()
        far = 1 - side
        cross_out[r] = (
            proj[r, core * 2 + far].astype(F32) + proj_in[r, far].astype(F32)
        ).astype(BF16)
        outgoing.append(send(cross_out.at[r], cross_in.at[r], {"mp": partner}))

    for r in range(CHUNKS):
        own = (
            ffn_mid[span(r), own_cols].astype(F32)
            + proj[r, core * 2 + side].astype(F32)
            + proj_in[r, side].astype(F32)
        )
        outgoing[r].wait_recv()
        mid = (own + cross_in[r].astype(F32)).astype(BF16)
        padded[HALO + r * size : HALO + (r + 1) * size, :] = mid.astype(F32)
        if r == 0:
            edge_out[0] = mid[:HALO]
            back = send(edge_out.at[0], edge_in.at[0], {"tm": previous})
        if r == CHUNKS - 1:
            edge_out[1] = mid[size - HALO :]
            ahead = send(edge_out.at[1], edge_in.at[1], {"tm": following})
    place = lax.rem(group, REC_SHARDS)
    starts = jnp.logical_or(place == REC_SHARDS // 2, group == 0)
    ends = jnp.logical_or(place == REC_SHARDS // 2 - 1, group == groups - 1)
    back.wait_recv()
    padded[HALO + rows :, :] = edge_in[0].astype(F32) * jnp.where(ends, 0.0, 1.0)
    ahead.wait_recv()
    padded[:HALO, :] = edge_in[1].astype(F32) * jnp.where(starts, 0.0, 1.0)

    block = min(64, rows)
    for c in range(width // LANES):
        cols = slice(c * LANES, (c + 1) * LANES)

        @pl.loop(0, rows // block)
        def _(i):
            base = pl.multiple_of(i * block, block)
            near = padded[pl.ds(base, block + 2 * HALO), cols]
            total = jnp.zeros((block, LANES), F32)
            for shift in range(8):
                moved = near
                if shift:
                    moved = pltpu.roll(near, block + 2 * HALO - shift, 0)
                for up in range(0, 2 * HALO, 8):
                    tap = up + shift - 1
                    if 0 <= tap < KERNEL:
                        total = total + taps[tap : tap + 1, cols] * moved[up : up + block]
            mid = near[HALO : HALO + block]
            out[pl.ds(base, block), cols] = (
                mid + total / (1.0 + jnp.exp(-total))
            ).astype(BF16)

    for copy in copies:
        copy.wait_send()


def body(
    frames, ffn_gain, w_up, w_down, ln_gain, w_qkv, w_out, conv_kernel, left_groups, start_offset
):
    rows, width = frames.shape
    d_model = w_up.shape[0]
    hidden = w_up.shape[1]
    size = rows // CHUNKS
    pairs = CHUNKS * (3 + 1 + 1 + 1 + LEFT + 1 + 1) + 2
    anywhere = pl.BlockSpec(memory_space=pl.ANY)
    in_vmem = pl.BlockSpec(memory_space=pltpu.VMEM)
    in_smem = pl.BlockSpec(memory_space=pltpu.SMEM)
    return pl.pallas_call(
        block_kernel,
        out_shape=jax.ShapeDtypeStruct((rows, width), BF16),
        in_specs=[
            in_smem, in_smem, anywhere, in_vmem, anywhere, anywhere, in_vmem, anywhere, anywhere,
            in_vmem,
        ],
        out_specs=in_vmem,
        scratch_shapes=[
            pltpu.VMEM((rows, d_model), BF16),
            pltpu.VMEM(w_up.shape, BF16),
            pltpu.VMEM(w_down.shape, BF16),
            pltpu.VMEM((d_model, 3 * width), BF16),
            pltpu.VMEM(w_out.shape, BF16),
            pltpu.VMEM((size, hidden), BF16),
            pltpu.VMEM((size, d_model), BF16),
            pltpu.VMEM((CHUNKS, size, d_model), BF16),
            pltpu.VMEM((CHUNKS, size // 2, d_model), BF16),
            pltpu.VMEM((CHUNKS, size // 2, d_model), BF16),
            pltpu.VMEM((CHUNKS, size // 2, d_model), BF16),
            pltpu.VMEM((rows, d_model), BF16),
            pltpu.VMEM((rows, width), BF16),
            pltpu.VMEM((LEFT + 1, rows, 2 * width), BF16),
            pltpu.VMEM((width // HEAD_DIM, rows, (LEFT + 1) * rows), F32),
            pltpu.VMEM((rows, width), BF16),
            pltpu.VMEM((CHUNKS, 4, size, width), BF16),
            pltpu.VMEM((CHUNKS, 2, size, width), BF16),
            pltpu.VMEM((CHUNKS, size, width), BF16),
            pltpu.VMEM((CHUNKS, size, width), BF16),
            pltpu.VMEM((rows + 2 * HALO, width), F32),
            pltpu.VMEM((2, HALO, width), BF16),
            pltpu.VMEM((2, HALO, width), BF16),
            pltpu.SemaphoreType.DMA((5,)),
            pltpu.SemaphoreType.DMA((pairs,)),
            pltpu.SemaphoreType.DMA((pairs,)),
        ],
        compiler_params=pltpu.CompilerParams(
            collective_id=0, has_side_effects=True, vmem_limit_bytes=44 * 2**20
        ),
        cost_estimate=pl.CostEstimate(
            flops=2 * rows * d_model * (2 * hidden + 4 * width) + 8 * rows * rows * 4 * width,
            bytes_accessed=12 * 2**20,
            transcendentals=rows * rows * 24,
        ),
        name="conformer_block",
    )(
        left_groups, start_offset, frames, ffn_gain.reshape(1, -1), w_up, w_down,
        ln_gain.reshape(1, -1), w_qkv.reshape(d_model, 3 * width), w_out, conv_kernel,
    )


def solution(mesh):
    return jax.shard_map(
        body,
        mesh=mesh,
        in_specs=(
            P("tm", "mp"),
            P(),
            P(None, "mp"),
            P("mp", None),
            P(),
            P(None, None, "mp"),
            P("mp", None),
            P(None, "mp"),
            P("tm"),
            P("tm"),
        ),
        out_specs=P("tm", "mp"),
        check_vma=False,
    )
```

time: 256 us -> 128 us (0.50)
  the two profiles are of different devices: /device:TPU:80 before, /device:TPU:164 now
where the time goes in v1:
time: 128 us
  Pallas kernels  109 us (85%)
  local copies, waits for them, and re-layouts  17.5 us (14%)
  between operations  1.36 us (1%)
    pallas_call x1, Pallas kernels, body(): pl.pallas_call(block_kernel, out_shape=jax.ShapeDtypeStruct((rows, width)...  109 us
    unnamed x16, local copies, waits for them, and re-layouts  13.1 us
    reshape x1, local copies, waits for them, and re-layouts, body(): w_qkv.reshape(d_model, 3 * width)  4.39 us

profile of v1, /device:TPU:164, one launch (start us, length us, event | category | flops | bytes accessed | tf_op | source)
XLA Modules:
  0.0 127.9 jit_solution(1568110861268055910)
XLA Ops:
  0.0 6.1 %copy.12 = bf16[1536,3,384]{0,2,1:T(8,128)(2,1)} copy(bf16[1536,3,384]{2,0,1:T(8,128)(2,1)} %param.15) | data formatting | bytes 7077888 | tf_op args[5]
  6.1 0.0 copy-start.5
  6.1 0.0 copy-start.6
  6.1 4.4 %copy.13.w_qkv = bf16[1536,1152]{1,0:T(8,128)(2,1)S(1)} copy(bf16[1536,1152]{0,1:T(8,128)(2,1)} %bitcast.1) | data formatting | bytes 7077888 | tf_op jit(solution)/shard_map/reshape | solution.py:344
  10.5 0.0 copy-done.5
  10.5 0.0 copy-done.6
  11.8 0.0 copy-start
  11.9 1.7 %copy-done = bf16[1536,768]{1,0:T(8,128)(2,1)S(1)} copy-done((bf16[1536,768]{1,0:T(8,128)(2,1)S(1)}, bf16[1536,768]{1,0:T(8,128)(2,1)}, u32[]{:S(2)}) %copy-start) | copy-done | bytes 2359320
  13.5 0.0 copy-start.1
  13.5 1.7 %copy-done.1 = bf16[768,1536]{1,0:T(8,128)(2,1)S(1)} copy-done((bf16[768,1536]{1,0:T(8,128)(2,1)S(1)}, bf16[768,1536]{1,0:T(8,128)(2,1)}, u32[]{:S(2)}) %copy-start.1) | copy-done | bytes 2359320
  15.2 0.0 copy-start.2
  15.2 1.3 copy-done.2
  16.4 0.0 copy-start.3
  16.5 0.9 copy-done.3
  17.4 0.0 copy-start.4
  17.4 0.8 copy-done.4
  18.2 109.0 %conformer_block.1 = bf16[256,384]{1,0:T(8,128)(2,1)S(1)} custom-call(s32[1]{0:T(128)S(6)} %copy.15.left_ref, s32[1]{0:T(128)S(6)} %copy.16.offset_ref, bf16[256,384]{1,0:T(8,128)(2,1)S(1)} %copy-done.3, f32[1,1536]{1,0:T(1,128)S(1)} %reshape.9.ffn_gain, bf16[1536,768]{1,0:T(8,128)(2,1)S(1)} %copy-done, bf16[768,1536]{1,0:T(8,128)(2,1)S(1)} %copy-done.1, ...), custom_call_target="tpu_custom_call" | custom-call | flops 3221225472 | bytes 12582912 | tf_op jit(solution)/shard_map/conformer_block/pallas_call | solution.py:297
  127.2 0.7 copy.17
  (2 shorter events, 0.0 us)
Async XLA Ops:
  6.1 4.4 %copy-start.5 = (f32[1536]{0:T(1024)S(1)}, f32[1536]{0:T(1024)}, u32[]{:S(2)}) copy-start(f32[1536]{0:T(1024)} %param.14) | copy-start | bytes 18436
  6.1 4.4 %copy-start.6 = (f32[1536]{0:T(1024)S(1)}, f32[1536]{0:T(1024)}, u32[]{:S(2)}) copy-start(f32[1536]{0:T(1024)} %param.11) | copy-start | bytes 18436
  11.8 1.7 %copy-start = (bf16[1536,768]{1,0:T(8,128)(2,1)S(1)}, bf16[1536,768]{1,0:T(8,128)(2,1)}, u32[]{:S(2)}) copy-start(bf16[1536,768]{1,0:T(8,128)(2,1)} %w_up.1) | copy-start | bytes 7077892
  13.5 1.7 %copy-start.1 = (bf16[768,1536]{1,0:T(8,128)(2,1)S(1)}, bf16[768,1536]{1,0:T(8,128)(2,1)}, u32[]{:S(2)}) copy-start(bf16[768,1536]{1,0:T(8,128)(2,1)} %w_down.1) | copy-start | bytes 7077892
  15.2 1.3 copy-start.2
  16.4 0.9 copy-start.3
  17.4 0.8 copy-start.4

commit v2 on v1

--- a/solution.py
+++ b/solution.py
@@ -11,7 +11,8 @@
 KERNEL = 31
 LEFT = 3
 REC_SHARDS = 8
-CHUNKS = 2
+CHUNKS = 4
+FFN_CHUNKS = 2
 LANES = 128
 HALO = 16
 HIDDEN_STEP = 256
@@ -35,7 +36,7 @@
 def block_kernel(
     left_ref, offset_ref, frames, ffn_gain, w_up, w_down, ln_gain, w_qkv, w_out, taps, out,
     whole, up_v, down_v, qkv_v, out_v, hidden, normed, partial, partial_in, chip_out, chip_in,
-    ffn_mid, queries, kv, scores, context, proj, proj_in, cross_out, cross_in, padded,
+    ffn_mid, queries, keys, values, scores, context, proj, proj_in, cross_out, cross_in, padded,
     edge_out, edge_in, local_sem, send_sem, recv_sem,
 ):
     rows, width = frames.shape
@@ -88,27 +89,35 @@
     def shared(r):
         return pl.ds(pl.multiple_of(r * size + core * half, half), half)
 
+    per = CHUNKS // FFN_CHUNKS
+    tall = per * size
+
+    def wide(a):
+        return pl.ds(a * tall, tall)
+
     to_partner, to_sibling = [], []
-    for r in range(CHUNKS):
+    for a in range(FFN_CHUNKS):
         to_partner.append(
-            send(frames.at[span(r), :], whole.at[span(r), own_cols], {"mp": partner})
+            send(frames.at[wide(a), :], whole.at[wide(a), own_cols], {"mp": partner})
         )
         to_sibling.append(
-            send(frames.at[span(r), :], whole.at[span(r), own_cols], {"mp": sibling})
+            send(frames.at[wide(a), :], whole.at[wide(a), own_cols], {"mp": sibling})
         )
     own_frames.wait()
 
     partner_cols = pl.ds(pl.multiple_of(partner * width, LANES), width)
+    mine = pl.ds(pl.multiple_of(core * half, half), half)
+    theirs = pl.ds(pl.multiple_of((1 - core) * half, half), half)
     crossing = []
-    for r in range(CHUNKS):
-        to_partner[r].wait_recv()
+    for a in range(FFN_CHUNKS):
+        to_partner[a].wait_recv()
         passed_on = send(
-            whole.at[span(r), partner_cols], whole.at[span(r), partner_cols], {"mp": sibling}
-        )
-        to_sibling[r].wait_recv()
+            whole.at[wide(a), partner_cols], whole.at[wide(a), partner_cols], {"mp": sibling}
+        )
+        to_sibling[a].wait_recv()
         passed_on.wait_recv()
-        normed[...] = layer_norm(whole[span(r), :], ffn_gain[...])
-        if r == 0:
+        normed[...] = layer_norm(whole[wide(a), :], ffn_gain[...])
+        if a == 0:
             loads[0].wait()
 
         @pl.loop(0, up_v.shape[1] // HIDDEN_STEP)
@@ -117,27 +126,39 @@
             v = dot(normed[...], up_v[:, cols])
             hidden[:, cols] = (v / (1.0 + jnp.exp(-v))).astype(BF16)
 
-        if r == 0:
+        if a == 0:
             loads[1].wait()
 
         @pl.loop(0, d_model // HIDDEN_STEP)
         def _(j):
             cols = pl.ds(pl.multiple_of(j * HIDDEN_STEP, HIDDEN_STEP), HIDDEN_STEP)
-            partial[r, :, cols] = dot(hidden[...], down_v[:, cols]).astype(BF16)
-
-        mine = pl.ds(pl.multiple_of(core * half, half), half)
-        theirs = pl.ds(pl.multiple_of((1 - core) * half, half), half)
-        swap = send(partial.at[r, theirs, :], partial_in.at[r], {"mp": sibling})
+            product = dot(hidden[...], down_v[:, cols]).astype(BF16)
+            for i in range(per):
+                partial[a * per + i, :, cols] = product[i * size : (i + 1) * size]
+
+        both = pl.ds(a * per, per)
+        swap = send(partial.at[both, theirs, :], partial_in.at[both], {"mp": sibling})
         swap.wait_recv()
-        chip_out[r] = (partial[r, mine, :].astype(F32) + partial_in[r].astype(F32)).astype(BF16)
-        crossing.append(send(chip_out.at[r], chip_in.at[r], {"mp": partner}))
-
-    hops = {}
-
-    def hop(h, r):
+        for r in range(a * per, (a + 1) * per):
+            chip_out[r] = (
+                partial[r, mine, :].astype(F32) + partial_in[r].astype(F32)
+            ).astype(BF16)
+            crossing.append(send(chip_out.at[r], chip_in.at[r], {"mp": partner}))
+
+    hops, here = {}, set()
+
+    def arrive(part, h, r):
+        if (part, h, r) not in here:
+            here.add((part, h, r))
+            hops[part, h, r].wait_recv()
+
+    def hop(part, h, r):
         if h > 1:
-            hops[h - 1, r].wait_recv()
-        hops[h, r] = send(kv.at[h - 1, span(r), :], kv.at[h, span(r), :], {"tm": following})
+            arrive(part, h - 1, r)
+        held = (keys, values)[part]
+        hops[part, h, r] = send(
+            held.at[h - 1, span(r), :], held.at[h, span(r), :], {"tm": following}
+        )
 
     for r in range(CHUNKS):
         crossing[r].wait_recv()
@@ -145,21 +166,21 @@
         ffn_mid[shared(r), :] = (whole[shared(r), :].astype(F32) + 0.5 * total).astype(BF16)
         joined = send(ffn_mid.at[shared(r), :], ffn_mid.at[shared(r), :], {"mp": sibling})
         joined.wait_recv()
-        normed[...] = layer_norm(ffn_mid[span(r), :], ln_gain[...])
+        ready = layer_norm(ffn_mid[span(r), :], ln_gain[...])
+        normed[:size] = ready
         if r == 0:
             loads[2].wait()
-        for c in (1, 2):
-            cols = slice(c * width, (c + 1) * width)
-            kv[0, span(r), slice((c - 1) * width, c * width)] = dot(
-                normed[...], qkv_v[:, cols]
-            ).astype(BF16)
-        hop(1, r)
+        for part in range(2):
+            (keys, values)[part][0, span(r), :] = dot(normed[:size], qkv_v[1 + part]).astype(BF16)
+            hop(part, 1, r)
         queries[span(r), :] = (
-            dot(normed[...], qkv_v[:, 0:width]).astype(BF16) * (HEAD_DIM ** -0.5)
+            dot(normed[:size], qkv_v[0]).astype(BF16) * (HEAD_DIM ** -0.5)
         ).astype(BF16)
-        for h in range(2, LEFT + 1):
-            if r - h + 1 >= 0:
-                hop(h, r - h + 1)
+        if r < CHUNKS - 1:
+            for h in range(LEFT, 1, -1):
+                if r - h + 1 >= 0:
+                    for part in range(2):
+                        hop(part, h, r - h + 1)
 
     left = left_ref[0]
     offset = offset_ref[0]
@@ -175,38 +196,37 @@
         def _(p):
             cols = pl.ds(pl.multiple_of(p * LANES, LANES), LANES)
             pair = queries[:, cols]
-            keys = kv[d, :, cols]
+            seen = keys[d, :, cols]
             for odd in range(2):
                 picked = jnp.where(upper if odd else jnp.logical_not(upper), pair, 0)
-                s = dot(picked, keys, ((1,), (1,)))
+                s = dot(picked, seen, ((1,), (1,)))
                 if d > 0:
                     s = jnp.where(shown, s, NEVER)
                 scores[2 * p + odd, :, d * rows : (d + 1) * rows] = s
 
-    todo = [(h, r) for r in range(CHUNKS) for h in range(2, LEFT + 1) if r + h - 1 >= CHUNKS]
-    todo.sort(key=lambda item: (item[0] + item[1], item[1]))
-    late = [item for item in todo if item[0] + item[1] <= CHUNKS]
-    for item in late:
-        hop(*item)
+    last = CHUNKS - 1
+    stages = {1: ((3, last - 2), (2, last - 1), (2, last)), 2: ((3, last - 1), (3, last)), 3: ()}
     score(0)
-    rest = [item for item in todo if item not in late]
     for d in range(1, LEFT + 1):
-        for item in [i for i in rest if i[0] + i[1] == CHUNKS + d]:
-            hop(*item)
+        for h, r in stages[d]:
+            for part in range(2):
+                hop(part, h, r)
         for r in range(CHUNKS):
-            if (d + 1, r) not in hops:
-                hops[d, r].wait_recv()
+            arrive(0, d, r)
         score(d)
+    for d in range(1, LEFT + 1):
+        for r in range(CHUNKS):
+            arrive(1, d, r)
 
     lower = lax.broadcasted_iota(jnp.int32, (size, LANES), 1) < HEAD_DIM
-    swaps, outgoing = [], []
+    swaps, outgoing = {}, {}
     loads[3].wait()
-    for r in range(CHUNKS):
-
+    far = 1 - side
+
+    def attend(r):
         @pl.loop(0, width // LANES)
         def _(p):
             cols = pl.ds(pl.multiple_of(p * LANES, LANES), LANES)
-            val_cols = pl.ds(pl.multiple_of(width + p * LANES, LANES), LANES)
             found = []
             for odd in range(2):
                 s = scores[2 * p + odd, span(r), :]
@@ -215,7 +235,7 @@
                 e = e.astype(BF16)
                 acc = None
                 for d in range(LEFT + 1):
-                    term = dot(e[:, d * rows : (d + 1) * rows], kv[d, :, val_cols])
+                    term = dot(e[:, d * rows : (d + 1) * rows], values[d, :, cols])
                     acc = term if acc is None else acc + term
                 found.append(acc / norm)
             context[span(r), cols] = jnp.where(lower, found[0], found[1]).astype(BF16)
@@ -224,17 +244,23 @@
             proj[r, (k % 2) * 2 + k // 2] = dot(
                 context[span(r), :], out_v[:, k * width : (k + 1) * width]
             ).astype(BF16)
-        swap = send(
-            proj.at[r, pl.ds((1 - core) * 2, 2)], proj_in.at[r], {"mp": sibling}
-        )
-        swap.wait_recv()
-        far = 1 - side
+        swaps[r] = send(proj.at[r, pl.ds((1 - core) * 2, 2)], proj_in.at[r], {"mp": sibling})
+
+    def cross(r):
+        swaps[r].wait_recv()
         cross_out[r] = (
             proj[r, core * 2 + far].astype(F32) + proj_in[r, far].astype(F32)
         ).astype(BF16)
-        outgoing.append(send(cross_out.at[r], cross_in.at[r], {"mp": partner}))
-
-    for r in range(CHUNKS):
+        outgoing[r] = send(cross_out.at[r], cross_in.at[r], {"mp": partner})
+
+    order = [0, CHUNKS - 1] + list(range(1, CHUNKS - 1))
+    for i, r in enumerate(order):
+        attend(r)
+        if i:
+            cross(order[i - 1])
+    cross(order[-1])
+
+    for r in order:
         own = (
             ffn_mid[span(r), own_cols].astype(F32)
             + proj[r, core * 2 + side].astype(F32)
@@ -290,7 +316,7 @@
     d_model = w_up.shape[0]
     hidden = w_up.shape[1]
     size = rows // CHUNKS
-    pairs = CHUNKS * (3 + 1 + 1 + 1 + LEFT + 1 + 1) + 2
+    pairs = 4 * FFN_CHUNKS + CHUNKS * (1 + 1 + 2 * LEFT + 1 + 1) + 2
     anywhere = pl.BlockSpec(memory_space=pl.ANY)
     in_vmem = pl.BlockSpec(memory_space=pltpu.VMEM)
     in_smem = pl.BlockSpec(memory_space=pltpu.SMEM)
@@ -306,17 +332,18 @@
             pltpu.VMEM((rows, d_model), BF16),
             pltpu.VMEM(w_up.shape, BF16),
             pltpu.VMEM(w_down.shape, BF16),
-            pltpu.VMEM((d_model, 3 * width), BF16),
+            pltpu.VMEM((3, d_model, width), BF16),
             pltpu.VMEM(w_out.shape, BF16),
-            pltpu.VMEM((size, hidden), BF16),
-            pltpu.VMEM((size, d_model), BF16),
+            pltpu.VMEM((rows // FFN_CHUNKS, hidden), BF16),
+            pltpu.VMEM((rows // FFN_CHUNKS, d_model), BF16),
             pltpu.VMEM((CHUNKS, size, d_model), BF16),
             pltpu.VMEM((CHUNKS, size // 2, d_model), BF16),
             pltpu.VMEM((CHUNKS, size // 2, d_model), BF16),
             pltpu.VMEM((CHUNKS, size // 2, d_model), BF16),
             pltpu.VMEM((rows, d_model), BF16),
             pltpu.VMEM((rows, width), BF16),
-            pltpu.VMEM((LEFT + 1, rows, 2 * width), BF16),
+            pltpu.VMEM((LEFT + 1, rows, width), BF16),
+            pltpu.VMEM((LEFT + 1, rows, width), BF16),
             pltpu.VMEM((width // HEAD_DIM, rows, (LEFT + 1) * rows), F32),
             pltpu.VMEM((rows, width), BF16),
             pltpu.VMEM((CHUNKS, 4, size, width), BF16),
@@ -331,7 +358,7 @@
             pltpu.SemaphoreType.DMA((pairs,)),
         ],
         compiler_params=pltpu.CompilerParams(
-            collective_id=0, has_side_effects=True, vmem_limit_bytes=44 * 2**20
+            collective_id=0, has_side_effects=True, vmem_limit_bytes=60 * 2**20
         ),
         cost_estimate=pl.CostEstimate(
             flops=2 * rows * d_model * (2 * hidden + 4 * width) + 8 * rows * rows * 4 * width,
@@ -341,7 +368,7 @@
         name="conformer_block",
     )(
         left_groups, start_offset, frames, ffn_gain.reshape(1, -1), w_up, w_down,
-        ln_gain.reshape(1, -1), w_qkv.reshape(d_model, 3 * width), w_out, conv_kernel,
+        ln_gain.reshape(1, -1), jnp.transpose(w_qkv, (1, 0, 2)), w_out, conv_kernel,
     )
 
 

time: 128 us -> 116 us (0.906)
  the two profiles are of different devices: /device:TPU:164 before, /device:TPU:108 now
where the time goes in v2:
time: 116 us; the launch traced here: 115 us
  Pallas kernels  110 us (95%)
  local copies, waits for them, and re-layouts  4.2 us (4%)
  between operations  1.31 us (1%)
    pallas_call x1, Pallas kernels, body(): pl.pallas_call(block_kernel, out_shape=jax.ShapeDtypeStruct((rows, width)...  110 us

profile of v2, /device:TPU:108, one launch (start us, length us, event | category | flops | bytes accessed | tf_op | source)
XLA Modules:
  0.0 115.3 jit_solution(15198568874341115600)
XLA Ops:
  1.3 1.3 %reshape.6.ffn_gain = f32[1,1536]{1,0:T(1,128)} reshape(f32[1536]{0:T(1024)} %param.11) | data formatting | bytes 12288 | tf_op jit(solution)/shard_map/reshape | solution.py:370
  2.6 1.3 %reshape.7.ln_gain = f32[1,1536]{1,0:T(1,128)} reshape(f32[1536]{0:T(1024)} %param.14) | data formatting | bytes 12288 | tf_op jit(solution)/shard_map/reshape | solution.py:371
  3.9 109.8 %conformer_block.1 = bf16[256,384]{1,0:T(8,128)(2,1)} custom-call(s32[1]{0:T(128)S(6)} %copy.12.left_ref, s32[1]{0:T(128)S(6)} %copy.13.offset_ref, bf16[256,384]{1,0:T(8,128)(2,1)} %frames.1, f32[1,1536]{1,0:T(1,128)} %reshape.6.ffn_gain, bf16[1536,768]{1,0:T(8,128)(2,1)} %w_up.1, bf16[768,1536]{1,0:T(8,128)(2,1)} %w_down.1, f32[1,1536]{1,0:T(1,128)} %reshape.7.ln_gain, ...), custom_call_target="tpu_custom_call" | custom-call | flops 3221225472 | bytes 12582912 | tf_op jit(solution)/shard_map/conformer_block/pallas_call | solution.py:323
  113.7 1.6 %copy.14 = bf16[256,384]{1,0:T(8,128)(2,1)} copy(bf16[256,384]{1,0:T(8,128)(2,1)} %conformer_block.1) | data formatting | bytes 393216

commit v3 on v2

--- a/solution.py
+++ b/solution.py
@@ -12,7 +12,7 @@
 LEFT = 3
 REC_SHARDS = 8
 CHUNKS = 4
-FFN_CHUNKS = 2
+FFN_CHUNKS = 4
 LANES = 128
 HALO = 16
 HIDDEN_STEP = 256
@@ -34,10 +34,10 @@
 
 
 def block_kernel(
-    left_ref, offset_ref, frames, ffn_gain, w_up, w_down, ln_gain, w_qkv, w_out, taps, out,
+    left_ref, offset_ref, frames, ffn_gain_in, w_up, w_down, ln_gain_in, w_qkv, w_out, taps_in, out,
     whole, up_v, down_v, qkv_v, out_v, hidden, normed, partial, partial_in, chip_out, chip_in,
     ffn_mid, queries, keys, values, scores, context, proj, proj_in, cross_out, cross_in, padded,
-    edge_out, edge_in, local_sem, send_sem, recv_sem,
+    edge_out, edge_in, ffn_gain, ln_gain, taps, local_sem, send_sem, recv_sem,
 ):
     rows, width = frames.shape
     d_model = whole.shape[1]
@@ -53,22 +53,27 @@
     following = lax.rem(group + 1, groups)
     previous = lax.rem(group + groups - 1, groups)
 
-    loads = []
-    for i, (src, dst) in enumerate(
-        ((w_up, up_v), (w_down, down_v), (w_qkv, qkv_v), (w_out, out_v))
-    ):
-        loads.append(pltpu.make_async_copy(src, dst, local_sem.at[i]))
-    own_cols = pl.ds(pl.multiple_of(me * width, LANES), width)
-    own_frames = pltpu.make_async_copy(frames, whole.at[:, own_cols], local_sem.at[4])
-    own_frames.start()
-    for load in loads:
-        load.start()
-
     barrier = pltpu.get_barrier_semaphore()
     for target in ({"mp": sibling}, {"mp": partner}, {"tm": following}, {"tm": previous}):
         pl.semaphore_signal(
             barrier, inc=1, device_id=target, device_id_type=pl.DeviceIdType.MESH
         )
+
+    loads = []
+    for i, (src, dst) in enumerate(
+        (
+            (w_up, up_v), (w_down, down_v), (w_qkv, qkv_v), (w_out, out_v),
+            (ffn_gain_in, ffn_gain), (ln_gain_in, ln_gain), (taps_in, taps),
+        )
+    ):
+        loads.append(pltpu.make_async_copy(src, dst, local_sem.at[i]))
+    own_cols = pl.ds(pl.multiple_of(me * width, LANES), width)
+    own_frames = pltpu.make_async_copy(frames, whole.at[:, own_cols], local_sem.at[7])
+    own_frames.start()
+    loads[4].start()
+    for load in loads[:4] + loads[5:]:
+        load.start()
+
     pl.semaphore_wait(barrier, 4)
 
     copies = []
@@ -108,7 +113,16 @@
     partner_cols = pl.ds(pl.multiple_of(partner * width, LANES), width)
     mine = pl.ds(pl.multiple_of(core * half, half), half)
     theirs = pl.ds(pl.multiple_of((1 - core) * half, half), half)
-    crossing = []
+    crossing, given = [], []
+
+    def exchange(a):
+        given[a].wait_recv()
+        for r in range(a * per, (a + 1) * per):
+            chip_out[r] = (
+                partial[r, mine, :].astype(F32) + partial_in[r].astype(F32)
+            ).astype(BF16)
+            crossing.append(send(chip_out.at[r], chip_in.at[r], {"mp": partner}))
+
     for a in range(FFN_CHUNKS):
         to_partner[a].wait_recv()
         passed_on = send(
@@ -116,7 +130,9 @@
         )
         to_sibling[a].wait_recv()
         passed_on.wait_recv()
-        normed[...] = layer_norm(whole[wide(a), :], ffn_gain[...])
+        if a == 0:
+            loads[4].wait()
+        normed[...] = layer_norm(whole[wide(a), :], ffn_gain[...].reshape(1, d_model))
         if a == 0:
             loads[0].wait()
 
@@ -137,13 +153,10 @@
                 partial[a * per + i, :, cols] = product[i * size : (i + 1) * size]
 
         both = pl.ds(a * per, per)
-        swap = send(partial.at[both, theirs, :], partial_in.at[both], {"mp": sibling})
-        swap.wait_recv()
-        for r in range(a * per, (a + 1) * per):
-            chip_out[r] = (
-                partial[r, mine, :].astype(F32) + partial_in[r].astype(F32)
-            ).astype(BF16)
-            crossing.append(send(chip_out.at[r], chip_in.at[r], {"mp": partner}))
+        given.append(send(partial.at[both, theirs, :], partial_in.at[both], {"mp": sibling}))
+        if a:
+            exchange(a - 1)
+    exchange(FFN_CHUNKS - 1)
 
     hops, here = {}, set()
 
@@ -166,7 +179,9 @@
         ffn_mid[shared(r), :] = (whole[shared(r), :].astype(F32) + 0.5 * total).astype(BF16)
         joined = send(ffn_mid.at[shared(r), :], ffn_mid.at[shared(r), :], {"mp": sibling})
         joined.wait_recv()
-        ready = layer_norm(ffn_mid[span(r), :], ln_gain[...])
+        if r == 0:
+            loads[5].wait()
+        ready = layer_norm(ffn_mid[span(r), :], ln_gain[...].reshape(1, d_model))
         normed[:size] = ready
         if r == 0:
             loads[2].wait()
@@ -275,6 +290,7 @@
         if r == CHUNKS - 1:
             edge_out[1] = mid[size - HALO :]
             ahead = send(edge_out.at[1], edge_in.at[1], {"tm": following})
+    loads[6].wait()
     place = lax.rem(group, REC_SHARDS)
     starts = jnp.logical_or(place == REC_SHARDS // 2, group == 0)
     ends = jnp.logical_or(place == REC_SHARDS // 2 - 1, group == groups - 1)
@@ -324,8 +340,8 @@
         block_kernel,
         out_shape=jax.ShapeDtypeStruct((rows, width), BF16),
         in_specs=[
-            in_smem, in_smem, anywhere, in_vmem, anywhere, anywhere, in_vmem, anywhere, anywhere,
-            in_vmem,
+            in_smem, in_smem, anywhere, anywhere, anywhere, anywhere, anywhere, anywhere, anywhere,
+            anywhere,
         ],
         out_specs=in_vmem,
         scratch_shapes=[
@@ -353,7 +369,10 @@
             pltpu.VMEM((rows + 2 * HALO, width), F32),
             pltpu.VMEM((2, HALO, width), BF16),
             pltpu.VMEM((2, HALO, width), BF16),
-            pltpu.SemaphoreType.DMA((5,)),
+            pltpu.VMEM((d_model,), F32),
+            pltpu.VMEM((d_model,), F32),
+            pltpu.VMEM((KERNEL, width), F32),
+            pltpu.SemaphoreType.DMA((8,)),
             pltpu.SemaphoreType.DMA((pairs,)),
             pltpu.SemaphoreType.DMA((pairs,)),
         ],
@@ -367,8 +386,8 @@
         ),
         name="conformer_block",
     )(
-        left_groups, start_offset, frames, ffn_gain.reshape(1, -1), w_up, w_down,
-        ln_gain.reshape(1, -1), jnp.transpose(w_qkv, (1, 0, 2)), w_out, conv_kernel,
+        left_groups, start_offset, frames, ffn_gain, w_up, w_down,
+        ln_gain, jnp.transpose(w_qkv, (1, 0, 2)), w_out, conv_kernel,
     )
 
 

time: 116 us -> 102 us (0.88)
  the two profiles are of different devices: /device:TPU:108 before, /device:TPU:1 now
where the time goes in v3:
time: 102 us
  Pallas kernels  99.2 us (97%)
  local copies, waits for them, and re-layouts  1.62 us (2%)
  between operations  1.3 us (1%)
    pallas_call x1, Pallas kernels, body(): pl.pallas_call(block_kernel, out_shape=jax.ShapeDtypeStruct((rows, width)...  99.2 us

profile of v3, /device:TPU:1, one launch (start us, length us, event | category | flops | bytes accessed | tf_op | source)
XLA Modules:
  0.0 102.1 jit_solution(10396118221702065791)
XLA Ops:
  1.3 99.2 %conformer_block.1 = bf16[256,384]{1,0:T(8,128)(2,1)} custom-call(s32[1]{0:T(128)S(6)} %copy.12.left_ref, s32[1]{0:T(128)S(6)} %copy.13.offset_ref, bf16[256,384]{1,0:T(8,128)(2,1)} %frames.1, f32[1536]{0:T(1024)} %ffn_gain_in.1, bf16[1536,768]{1,0:T(8,128)(2,1)} %w_up.1, bf16[768,1536]{1,0:T(8,128)(2,1)} %w_down.1, f32[1536]{0:T(1024)} %ln_gain_in.1, ...), custom_call_target="tpu_custom_call" | custom-call | flops 3221225472 | bytes 12582912 | tf_op jit(solution)/shard_map/conformer_block/pallas_call | solution.py:339
  100.5 1.6 %copy.14 = bf16[256,384]{1,0:T(8,128)(2,1)} copy(bf16[256,384]{1,0:T(8,128)(2,1)} %conformer_block.1) | data formatting | bytes 393216

commit v4 on v3

--- a/solution.py
+++ b/solution.py
@@ -37,7 +37,7 @@
     left_ref, offset_ref, frames, ffn_gain_in, w_up, w_down, ln_gain_in, w_qkv, w_out, taps_in, out,
     whole, up_v, down_v, qkv_v, out_v, hidden, normed, partial, partial_in, chip_out, chip_in,
     ffn_mid, queries, keys, values, scores, context, proj, proj_in, cross_out, cross_in, padded,
-    edge_out, edge_in, ffn_gain, ln_gain, taps, local_sem, send_sem, recv_sem,
+    edge_out, edge_in, ffn_gain, ln_gain, taps, ready, local_sem, send_sem, recv_sem,
 ):
     rows, width = frames.shape
     d_model = whole.shape[1]
@@ -154,9 +154,7 @@
 
         both = pl.ds(a * per, per)
         given.append(send(partial.at[both, theirs, :], partial_in.at[both], {"mp": sibling}))
-        if a:
-            exchange(a - 1)
-    exchange(FFN_CHUNKS - 1)
+        exchange(a)
 
     hops, here = {}, set()
 
@@ -173,30 +171,34 @@
             held.at[h - 1, span(r), :], held.at[h, span(r), :], {"tm": following}
         )
 
+    def query(r):
+        queries[span(r), :] = (
+            dot(ready[span(r), :], qkv_v[0]).astype(BF16) * (HEAD_DIM ** -0.5)
+        ).astype(BF16)
+
     for r in range(CHUNKS):
         crossing[r].wait_recv()
         total = chip_out[r].astype(F32) + chip_in[r].astype(F32)
         ffn_mid[shared(r), :] = (whole[shared(r), :].astype(F32) + 0.5 * total).astype(BF16)
         joined = send(ffn_mid.at[shared(r), :], ffn_mid.at[shared(r), :], {"mp": sibling})
+        if r > 0:
+            query(r - 1)
         joined.wait_recv()
         if r == 0:
             loads[5].wait()
-        ready = layer_norm(ffn_mid[span(r), :], ln_gain[...].reshape(1, d_model))
-        normed[:size] = ready
+        ready[span(r), :] = layer_norm(ffn_mid[span(r), :], ln_gain[...].reshape(1, d_model))
         if r == 0:
             loads[2].wait()
         for part in range(2):
-            (keys, values)[part][0, span(r), :] = dot(normed[:size], qkv_v[1 + part]).astype(BF16)
+            (keys, values)[part][0, span(r), :] = dot(ready[span(r), :], qkv_v[1 + part]).astype(BF16)
             hop(part, 1, r)
-        queries[span(r), :] = (
-            dot(normed[:size], qkv_v[0]).astype(BF16) * (HEAD_DIM ** -0.5)
-        ).astype(BF16)
         if r < CHUNKS - 1:
             for h in range(LEFT, 1, -1):
                 if r - h + 1 >= 0:
                     for part in range(2):
                         hop(part, h, r - h + 1)
 
+    query(CHUNKS - 1)
     left = left_ref[0]
     offset = offset_ref[0]
     position = lax.broadcasted_iota(jnp.int32, (rows, rows), 1)
@@ -372,6 +374,7 @@
             pltpu.VMEM((d_model,), F32),
             pltpu.VMEM((d_model,), F32),
             pltpu.VMEM((KERNEL, width), F32),
+            pltpu.VMEM((rows, d_model), BF16),
             pltpu.SemaphoreType.DMA((8,)),
             pltpu.SemaphoreType.DMA((pairs,)),
             pltpu.SemaphoreType.DMA((pairs,)),

time: 102 us -> 100 us (0.980)
  Pallas kernels: 99.2 us -> 97.1 us
    pallas_call x1, Pallas kernels: 99.2 us -> 97.1 us  [body(): pl.pallas_call(block_kernel, out_shape=jax.ShapeDtypeStruct((rows, width)...]
where the time goes in v4:
time: 100 us
  Pallas kernels  97.1 us (97%)
  local copies, waits for them, and re-layouts  1.62 us (2%)
  between operations  1.3 us (1%)
    pallas_call x1, Pallas kernels, body(): pl.pallas_call(block_kernel, out_shape=jax.ShapeDtypeStruct((rows, width)...  97.1 us

profile of v4, /device:TPU:1, one launch (start us, length us, event | category | flops | bytes accessed | tf_op | source)
XLA Modules:
  0.0 100.0 jit_solution(3819797516957596160)
XLA Ops:
  1.3 97.1 %conformer_block.1 = bf16[256,384]{1,0:T(8,128)(2,1)} custom-call(s32[1]{0:T(128)S(6)} %copy.12.left_ref, s32[1]{0:T(128)S(6)} %copy.13.offset_ref, bf16[256,384]{1,0:T(8,128)(2,1)} %frames.1, f32[1536]{0:T(1024)} %ffn_gain_in.1, bf16[1536,768]{1,0:T(8,128)(2,1)} %w_up.1, bf16[768,1536]{1,0:T(8,128)(2,1)} %w_down.1, f32[1536]{0:T(1024)} %ln_gain_in.1, ...), custom_call_target="tpu_custom_call" | custom-call | flops 3221225472 | bytes 12582912 | tf_op jit(solution)/shard_map/conformer_block/pallas_call | solution.py:341
  98.4 1.6 %copy.14 = bf16[256,384]{1,0:T(8,128)(2,1)} copy(bf16[256,384]{1,0:T(8,128)(2,1)} %conformer_block.1) | data formatting | bytes 393216
